TPU v7x, 32 devices: a whole 2x2x4 slice. The times are simulated.
32 devices in a mesh: group: 2 (over y), ctx: 8 (over z, x), head: 2 (over core).
Axes of the slice: x: 2, y: 2, z: 4, core: 2. Of those that a mesh axis runs over, the one named last changes fastest.
Arguments:
- queries: bfloat16 [4096, 4096], P(('group', 'ctx'), 'head'), parts along dimension 0, may hold values from -7 to 7
- keys: bfloat16 [4096, 1024], P(('group', 'ctx'), 'head'), parts along dimension 0, may hold values from -4 to 4
- values: bfloat16 [4096, 1024], P(('group', 'ctx'), 'head'), parts along dimension 0, may hold values from -24 to 24
- doc_of_block: int32 [32], P('group'), parts along dimension 0, may hold values from 0 to 4, never falling along the last dimension, each value on 1 to 8 neighbouring positions
- out_weight: bfloat16 [4096, 4096], P('ctx', 'head'), may hold values from -0.09375 to 0.09375
Outputs:
- mixed: bfloat16 [4096, 4096], P(('group', 'ctx'), 'head'), parts along dimension 0
There are 2 independent parts, one for each index of `group`. A program takes and returns all parts, laid end to end along the dimension named above; an argument that names none is the same for every part. Nothing has to cross between parts.
Inputs may be any that keep to these rules, and one draw needn't show every extreme that they name: `doc_of_block`: blocks of one document are consecutive, and a document covers at most 8 blocks.
All inputs are finite; a program needn't handle non-finite values.
Results may differ from a plain program's by a relative error of at most 0.006.
Values may be sent and summed in bfloat16 or wider, within the bound.
A program may use at most 64 MiB of HBM per device.

v0:
```python
import math

import jax
import jax.numpy as jnp
from jax import lax
from jax.sharding import PartitionSpec as P

HEAD_SIZE = 128
BLOCK_TOKENS = 128


def passed_along(array, axis, by):
    peers = lax.axis_size(axis)
    pairs = [(i, i + by) for i in range(peers) if 0 <= i + by < peers]
    return lax.ppermute(array, axis, pairs)


def lookup_docs(positions, doc_of_block):
    block_ids = jnp.floor_divide(positions, BLOCK_TOKENS)
    table_ids = jnp.arange(doc_of_block.shape[0], dtype=jnp.int32)
    matches = block_ids[:, None] == table_ids[None, :]
    return jnp.max(jnp.where(matches, doc_of_block[None, :], -1), axis=1)


def update(state_now, query_head_rows, key_piece, value_piece, visible):
    running_max, summed, totals = state_now
    rows_here = key_piece.shape[0]
    kv_heads = query_head_rows.shape[1]
    key_head_rows = key_piece.reshape(rows_here, kv_heads, HEAD_SIZE)
    value_head_rows = value_piece.reshape(rows_here, kv_heads, HEAD_SIZE)
    score_scale = 1.0 / math.sqrt(HEAD_SIZE)
    scores = (
        jnp.einsum(
            "qhgd,khd->hgqk", query_head_rows, key_head_rows, preferred_element_type=jnp.float32
        )
        * score_scale
    )
    scores = jnp.where(visible, scores, -1e30)
    new_max = jnp.maximum(running_max, jnp.max(scores, axis=-1))
    weights = jnp.where(visible, jnp.exp(scores - new_max[..., None]), 0.0)
    rescale = jnp.exp(running_max - new_max)
    products = jnp.einsum(
        "hgqk,khd->hgqd",
        weights.astype(jnp.bfloat16),
        value_head_rows,
        preferred_element_type=jnp.float32,
    )
    summed = summed * rescale[..., None] + products
    totals = totals * rescale + jnp.sum(weights, axis=-1)
    return (new_max, summed, totals)


def fresh_state(kv_heads, group_width, rows_here):
    return (
        jnp.full((kv_heads, group_width, rows_here), -1e30, jnp.float32),
        jnp.zeros((kv_heads, group_width, rows_here, HEAD_SIZE), jnp.float32),
        jnp.zeros((kv_heads, group_width, rows_here), jnp.float32),
    )


def finish(state_now, rows_here, q_heads):
    running_max, summed, totals = state_now
    attended = summed / totals[..., None]
    return (
        jnp.transpose(attended, (2, 0, 1, 3))
        .reshape(rows_here, q_heads * HEAD_SIZE)
        .astype(jnp.bfloat16)
    )


def per_device(queries, keys, values, doc_of_block, out_weight):
    tok_rows = queries.shape[0]
    kv_heads = keys.shape[1] // HEAD_SIZE
    q_heads = queries.shape[1] // HEAD_SIZE
    group_width = q_heads // kv_heads
    ctx_count = lax.axis_size("ctx")
    reach_devs = min(8, ctx_count // 2)
    ctx_index = lax.axis_index("ctx")
    query_start = ctx_index * tok_rows
    query_pos = query_start + jnp.arange(tok_rows, dtype=jnp.int32)
    query_doc = lookup_docs(query_pos, doc_of_block)
    query_head_rows = queries.reshape(tok_rows, kv_heads, group_width, HEAD_SIZE)

    def attend(state_now, key_piece, value_piece, key_start):
        key_pos = key_start + jnp.arange(key_piece.shape[0], dtype=jnp.int32)
        key_doc = lookup_docs(key_pos, doc_of_block)
        visible = (key_doc[None, :] == query_doc[:, None]) & (
            key_pos[None, :] <= query_pos[:, None]
        )
        return update(state_now, query_head_rows, key_piece, value_piece, visible)

    initial_state = fresh_state(kv_heads, group_width, tok_rows)
    state_now = attend(initial_state, keys, values, query_start)
    for distance in range(1, reach_devs + 1):
        prior_keys, prior_values = passed_along((keys, values), "ctx", distance)
        state_now = attend(state_now, prior_keys, prior_values, query_start - distance * tok_rows)
    attended = finish(state_now, tok_rows, q_heads)
    features = lax.all_gather(attended, "head", axis=1, tiled=True)
    mixed = jnp.dot(
        features,
        lax.all_gather(out_weight, "ctx", axis=0, tiled=True),
        preferred_element_type=jnp.float32,
    )
    return mixed.astype(jnp.bfloat16)


def solution(mesh):
    return jax.shard_map(
        per_device,
        mesh=mesh,
        in_specs=(
            P(("group", "ctx"), "head"),
            P(("group", "ctx"), "head"),
            P(("group", "ctx"), "head"),
            P("group"),
            P("ctx", "head"),
        ),
        out_specs=P(("group", "ctx"), "head"),
        check_vma=False,
    )
```

profile of v0, /device:TPU:17, one launch (start us, length us, event | category | flops | bytes accessed | tf_op | source)
XLA Modules:
  0.0 349.7 jit_solution(2587613839477615480)
XLA Ops:
  6.5 1.1 copy.50
  7.6 1.3 collective-permute-start.6
  8.9 4.1 %collective-permute-start.4 = (bf16[256,512]{0,1:T(8,128)(2,1)S(1)}, bf16[256,512]{0,1:T(8,128)(2,1)S(1)}, u32[]{:S(2)}, u32[]{:S(2)}) collective-permute-start(bf16[256,512]{0,1:T(8,128)(2,1)S(1)} %copy.50), channel_id=1, source_target_pairs={{0,6},{2,8},{4,10},{6,12},{8,14},{1,7},{3,9},{5,11},{7,13},{9,15},... | collective-permute-start | bytes 786440 | tf_op jit(solution)/shard_map/ppermute | solution.py:15
  13.1 1.9 collective-permute-start.2
  15.0 1.9 collective-permute-start
  16.9 1.9 collective-permute-start.1
  18.9 1.0 reshape.264
  19.9 0.0 copy-start.4
  19.9 1.9 copy.87
  21.8 1.8 reshape.265
  23.6 0.8 select_reduce_fusion
  24.4 0.5 compare_and_fusion.4
  24.9 1.0 fusion
  25.9 0.0 collective-permute-done.6
  25.9 1.9 collective-permute-start.3
  27.9 2.9 fusion.4
  30.8 0.0 collective-permute-done.4
  30.8 7.3 %collective-permute-start.5 = (bf16[256,512]{1,0:T(8,128)(2,1)S(1)}, bf16[256,512]{1,0:T(8,128)(2,1)S(1)}, u32[]{:S(2)}, u32[]{:S(2)}) collective-permute-start(bf16[256,512]{1,0:T(8,128)(2,1)S(1)} %copy-done.4), channel_id=1, source_target_pairs={{0,6},{2,8},{4,10},{6,12},{8,14},{1,7},{3,9},{5,11},{7,13},{9,15},... | collective-permute-start | bytes 786440 | tf_op jit(solution)/shard_map/ppermute | solution.py:15
  38.2 3.0 fusion.3
  41.1 0.0 collective-permute-done.2
  41.1 1.5 collective-permute-start.7
  42.6 3.0 fusion.2
  45.6 3.2 collective-permute-done
  48.8 1.0 fusion.1
  49.8 1.0 fusion.5
  50.9 2.5 fusion.23
  53.4 1.0 fusion.7
  54.5 10.1 %collective-permute-done.1 = bf16[256,512]{1,0:T(8,128)(2,1)S(1)} collective-permute-done((bf16[256,512]{1,0:T(8,128)(2,1)}, bf16[256,512]{1,0:T(8,128)(2,1)S(1)}, u32[]{:S(2)}, u32[]{:S(2)}) %collective-permute-start.1) | collective-permute-done | bytes 262176 | tf_op jit(solution)/shard_map/ppermute | solution.py:15
  64.6 0.1 copy.53
  64.7 4.9 %fusion.21 = f32[4,4,256,128]{2,3,1,0:T(8,128)} fusion(bf16[256,4,128,1]{0,2,3,1:T(8,128)(2,1)S(1)} %bitcast.249, f32[4,256,256,4]{2,1,3,0:T(8,128)} %copy-done.3, f32[4,4,256]{2,1,0:T(4,128)S(1)} %get-tuple-element.17, pred[256,256]{0,1:T(8,128)(4,1)S(1)} %get-tuple-element.22), kind=kOutput, calls=%fused_computation.29 | convolution fusion | flops 273678336 | bytes 6635520 | tf_op jit(solution)/shard_map/hgqk,khd->hgqd/dot_general | solution.py:42
  69.6 1.0 fusion.9
  70.6 0.0 collective-permute-done.3
  70.6 1.1 copy.58
  71.7 4.9 %fusion.19 = f32[4,4,256,128]{2,3,1,0:T(8,128)} fusion(bf16[256,4,128,1]{0,2,3,1:T(8,128)(2,1)S(1)} %bitcast.250, f32[4,256,256,4]{2,1,3,0:T(8,128)} %get-tuple-element.31, f32[4,4,256]{2,1,0:T(4,128)S(1)} %get-tuple-element.16, pred[256,256]{0,1:T(8,128)(4,1)S(1)} %get-tuple-element.24), kind=kOutput, calls=%fused_computation.28 | convolution fusion | flops 273678336 | bytes 6635520 | tf_op jit(solution)/shard_map/hgqk,khd->hgqd/dot_general | solution.py:42
  76.6 1.0 fusion.11
  77.7 0.0 collective-permute-done.5
  77.7 0.1 copy.63
  77.8 4.9 %fusion.17 = f32[4,4,256,128]{2,3,1,0:T(8,128)} fusion(bf16[256,4,128,1]{0,2,3,1:T(8,128)(2,1)S(1)} %bitcast.251, f32[4,256,256,4]{2,1,3,0:T(8,128)} %get-tuple-element.29, f32[4,4,256]{2,1,0:T(4,128)S(1)} %get-tuple-element.15, pred[256,256]{0,1:T(8,128)(4,1)S(1)} %get-tuple-element.23), kind=kOutput, calls=%fused_computation.27 | convolution fusion | flops 273678336 | bytes 6635520 | tf_op jit(solution)/shard_map/hgqk,khd->hgqd/dot_general | solution.py:42
  82.7 1.0 fusion.13
  83.8 0.0 collective-permute-done.7
  83.8 0.4 copy.68
  84.2 7.4 %fusion.26 = bf16[256,4,4,128]{0,3,2,1:T(8,128)(2,1)} fusion(f32[4,4,256,128]{2,3,1,0:T(8,128)} %fusion.17, f32[4,4,256,128]{2,3,1,0:T(8,128)} %fusion.19, f32[4,4,256,128]{2,3,1,0:T(8,128)} %fusion.21, f32[4,4,256,128]{2,3,1,0:T(8,128)} %fusion.23, f32[256,4,4]{0,2,1:T(4,128)S(1)} %get-tuple-element.10, f32[256,4,4]{0,2,1:T(4,128)S(1)} %get-tuple-element.13, ...), kind=kOutput, calls=%fused_computation.33 | convolution fusion | flops 279445504 | bytes 14073856 | tf_op jit(solution)/shard_map/hgqk,khd->hgqd/dot_general | solution.py:42
  91.5 0.0 all-gather.3.cloned.1.call-update
  91.6 0.0 all-gather.5.cloned.1.call-start
  91.6 0.7 all-gather.5.cloned.1.call-update
  92.3 9.7 %all-gather.3.cloned.1.call-done = bf16[256,4096]{0,1:T(8,128)(2,1)} async-done(((bf16[256,2048]{0,1:T(8,128)(2,1)}), bf16[256,4096]{0,1:T(8,128)(2,1)}) %all-gather.3.cloned.1.call-update) | async-done | bytes 2097168 | tf_op jit(solution)/shard_map/all_gather | solution.py:98
  102.1 228.9 %all-gather.5.cloned.1.call-done = bf16[4096,2048]{1,0:T(8,128)(2,1)} async-done(((bf16[512,2048]{1,0:T(8,128)(2,1)}), bf16[4096,2048]{1,0:T(8,128)(2,1)}) %all-gather.5.cloned.1.call-update) | async-done | bytes 16777232 | tf_op jit(solution)/shard_map/all_gather | solution.py:101
  331.0 11.9 %convolution_convert_fusion = bf16[256,2048]{1,0:T(8,128)(2,1)} fusion(bf16[256,4096]{0,1:T(8,128)(2,1)} %all-gather.3.cloned.1.call-done, bf16[4096,2048]{1,0:T(8,128)(2,1)} %all-gather.5.cloned.1.call-done), kind=kOutput, calls=%fused_computation.25 | convolution fusion | flops 4295491584 | bytes 19922944 | tf_op jit(solution)/shard_map/dot_general | solution.py:99
  (19 shorter events, 0.1 us)
Async XLA Ops:
  6.5 95.5 %all-gather.3.cloned.1.call-start = ((), (), s32[]{:S(2)}) async-start(), calls=%async_computation | async-start | bytes 3145728 | tf_op jit(solution)/shard_map/all_gather | solution.py:98
  7.6 18.3 %collective-permute-start.6 = (bf16[256,512]{0,1:T(8,128)(2,1)S(1)}, bf16[256,512]{0,1:T(8,128)(2,1)S(1)}, u32[]{:S(2)}, u32[]{:S(2)}) collective-permute-start(bf16[256,512]{0,1:T(8,128)(2,1)S(1)} %copy.50), channel_id=1, source_target_pairs={{0,8},{2,10},{4,12},{6,14},{1,9},{3,11},{5,13},{7,15},{16,24},{18,... | collective-permute-start | bytes 786440 | tf_op jit(solution)/shard_map/ppermute | solution.py:15
  8.9 21.9 %collective-permute-start.4 = (bf16[256,512]{0,1:T(8,128)(2,1)S(1)}, bf16[256,512]{0,1:T(8,128)(2,1)S(1)}, u32[]{:S(2)}, u32[]{:S(2)}) collective-permute-start(bf16[256,512]{0,1:T(8,128)(2,1)S(1)} %copy.50), channel_id=1, source_target_pairs={{0,6},{2,8},{4,10},{6,12},{8,14},{1,7},{3,9},{5,11},{7,13},{9,15},... | collective-permute-start | bytes 786440 | tf_op jit(solution)/shard_map/ppermute | solution.py:15
  13.1 28.1 %collective-permute-start.2 = (bf16[256,512]{0,1:T(8,128)(2,1)S(1)}, bf16[256,512]{0,1:T(8,128)(2,1)S(1)}, u32[]{:S(2)}, u32[]{:S(2)}) collective-permute-start(bf16[256,512]{0,1:T(8,128)(2,1)S(1)} %copy.50), channel_id=1, source_target_pairs={{0,4},{2,6},{4,8},{6,10},{8,12},{10,14},{1,5},{3,7},{5,9},{7,11},{... | collective-permute-start | bytes 786440 | tf_op jit(solution)/shard_map/ppermute | solution.py:15
  15.0 33.8 %collective-permute-start = (bf16[256,512]{0,1:T(8,128)(2,1)S(1)}, bf16[256,512]{0,1:T(8,128)(2,1)S(1)}, u32[]{:S(2)}, u32[]{:S(2)}) collective-permute-start(bf16[256,512]{0,1:T(8,128)(2,1)S(1)} %copy.50), channel_id=1, source_target_pairs={{0,2},{2,4},{4,6},{6,8},{8,10},{10,12},{12,14},{1,3},{3,5},{5,7},{... | collective-permute-start | bytes 786440 | tf_op jit(solution)/shard_map/ppermute | solution.py:15
  16.9 47.6 %collective-permute-start.1 = (bf16[256,512]{1,0:T(8,128)(2,1)}, bf16[256,512]{1,0:T(8,128)(2,1)S(1)}, u32[]{:S(2)}, u32[]{:S(2)}) collective-permute-start(bf16[256,512]{1,0:T(8,128)(2,1)} %param.7), channel_id=1, source_target_pairs={{0,2},{2,4},{4,6},{6,8},{8,10},{10,12},{12,14},{1,3},{3,5},{5,7},{... | collective-permute-start | bytes 786440 | tf_op jit(solution)/shard_map/ppermute | solution.py:15
  19.9 6.1 %copy-start.4 = (bf16[256,512]{1,0:T(8,128)(2,1)S(1)}, bf16[256,512]{1,0:T(8,128)(2,1)}, u32[]{:S(2)}) copy-start(bf16[256,512]{1,0:T(8,128)(2,1)} %param.7) | copy-start | bytes 786436
  25.9 44.7 %collective-permute-start.3 = (bf16[256,512]{1,0:T(8,128)(2,1)S(1)}, bf16[256,512]{1,0:T(8,128)(2,1)}, u32[]{:S(2)}, u32[]{:S(2)}) collective-permute-start(bf16[256,512]{1,0:T(8,128)(2,1)S(1)} %copy-done.4), channel_id=1, source_target_pairs={{0,4},{2,6},{4,8},{6,10},{8,12},{10,14},{1,5},{3,7},{5,9},{7,11},{... | collective-permute-start | bytes 786440 | tf_op jit(solution)/shard_map/ppermute | solution.py:15
  30.8 46.9 %collective-permute-start.5 = (bf16[256,512]{1,0:T(8,128)(2,1)S(1)}, bf16[256,512]{1,0:T(8,128)(2,1)S(1)}, u32[]{:S(2)}, u32[]{:S(2)}) collective-permute-start(bf16[256,512]{1,0:T(8,128)(2,1)S(1)} %copy-done.4), channel_id=1, source_target_pairs={{0,6},{2,8},{4,10},{6,12},{8,14},{1,7},{3,9},{5,11},{7,13},{9,15},... | collective-permute-start | bytes 786440 | tf_op jit(solution)/shard_map/ppermute | solution.py:15
  41.1 42.7 %collective-permute-start.7 = (bf16[256,512]{1,0:T(8,128)(2,1)S(1)}, bf16[256,512]{1,0:T(8,128)(2,1)S(1)}, u32[]{:S(2)}, u32[]{:S(2)}) collective-permute-start(bf16[256,512]{1,0:T(8,128)(2,1)S(1)} %copy-done.4), channel_id=1, source_target_pairs={{0,8},{2,10},{4,12},{6,14},{1,9},{3,11},{5,13},{7,15},{16,24},{18,... | collective-permute-start | bytes 786440 | tf_op jit(solution)/shard_map/ppermute | solution.py:15
  48.8 2.1 copy-start.5
  49.8 3.6 %copy-start.3 = (f32[4,256,256,4]{2,1,3,0:T(8,128)}, f32[4,256,256,4]{2,1,3,0:T(8,128)S(1)}, u32[]{:S(2)}) copy-start(f32[4,256,256,4]{2,1,3,0:T(8,128)S(1)} %get-tuple-element.33) | copy-start | bytes 12582916
  64.7 4.9 %copy-start.2 = (f32[4,256,256,4]{2,1,3,0:T(8,128)S(1)}, f32[4,256,256,4]{2,1,3,0:T(8,128)}, u32[]{:S(2)}) copy-start(f32[4,256,256,4]{2,1,3,0:T(8,128)} %get-tuple-element.31) | copy-start | bytes 12582916
  71.7 4.9 %copy-start.1 = (f32[4,256,256,4]{2,1,3,0:T(8,128)S(1)}, f32[4,256,256,4]{2,1,3,0:T(8,128)}, u32[]{:S(2)}) copy-start(f32[4,256,256,4]{2,1,3,0:T(8,128)} %get-tuple-element.29) | copy-start | bytes 12582916
  77.8 4.9 %copy-start = (f32[4,256,256,4]{2,1,3,0:T(8,128)S(1)}, f32[4,256,256,4]{2,1,3,0:T(8,128)}, u32[]{:S(2)}) copy-start(f32[4,256,256,4]{2,1,3,0:T(8,128)} %get-tuple-element.27) | copy-start | bytes 12582916
  91.6 239.4 %all-gather.5.cloned.1.call-start = ((), (), s32[]{:S(2)}) async-start(), calls=%async_computation.1 | async-start | bytes 18874368 | tf_op jit(solution)/shard_map/all_gather | solution.py:101
Sparse Core Ops, SparseCore 0:
  91.7 10.3 all-gather.2
  104.2 226.7 all-gather.4
where the time goes:
time: 353 us; the launch traced here: 350 us
  waiting for transfers between devices  253 us (72%)
  matrix products  47.3 us (13%)
  starting transfers between devices  22 us (6%)
  between operations  13.7 us (4%)
  local copies, waits for them, and re-layouts  7.46 us (2%)
  other arithmetic  6.66 us (2%)
    all_gather x1, waiting for transfers between devices, per_device(): lax.all_gather(out_weight, 'ctx', axis=0, tiled=True)  229 us
    dot_general x5, matrix products, update(): jnp.einsum('hgqk,khd->hgqd', weights.astype(jnp.bfloat16), value_head_row...  24.5 us
    ppermute x8, starting transfers between devices, passed_along(): return lax.ppermute(array, axis, pairs)  21.9 us
    ppermute x8, waiting for transfers between devices, passed_along(): return lax.ppermute(array, axis, pairs)  13.3 us
    dot_general x1, matrix products, per_device(): jnp.dot(features, lax.all_gather(out_weight, 'ctx', axis=0, tiled=True),...  11.9 us
    dot_general x5, matrix products, update(): jnp.einsum('qhgd,khd->hgqk', query_head_rows, key_head_rows, preferred_el...  10.8 us
    all_gather x1, waiting for transfers between devices, per_device(): features = lax.all_gather(attended, 'head', axis=1, tiled=True)  9.74 us
  transfers between devices with their start and end apart: 10, of which 4 were waited for; matrix products, arithmetic and copies ran while one was open for 12% of the time, Pallas kernels for 0%

commit v1 on v0

--- a/solution.py
+++ b/solution.py
@@ -76,6 +76,11 @@
     ctx_count = lax.axis_size("ctx")
     reach_devs = min(8, ctx_count // 2)
     ctx_index = lax.axis_index("ctx")
+    part_cols = out_weight.shape[1] // lax.axis_size("group")
+    weight_part = lax.dynamic_slice_in_dim(
+        out_weight, lax.axis_index("group") * part_cols, part_cols, 1
+    )
+    weight_part = lax.all_gather(weight_part, "ctx", axis=0, tiled=True)
     query_start = ctx_index * tok_rows
     query_pos = query_start + jnp.arange(tok_rows, dtype=jnp.int32)
     query_doc = lookup_docs(query_pos, doc_of_block)
@@ -95,13 +100,31 @@
         prior_keys, prior_values = passed_along((keys, values), "ctx", distance)
         state_now = attend(state_now, prior_keys, prior_values, query_start - distance * tok_rows)
     attended = finish(state_now, tok_rows, q_heads)
-    features = lax.all_gather(attended, "head", axis=1, tiled=True)
-    mixed = jnp.dot(
-        features,
-        lax.all_gather(out_weight, "ctx", axis=0, tiled=True),
-        preferred_element_type=jnp.float32,
-    )
-    return mixed.astype(jnp.bfloat16)
+    groups, heads = lax.axis_size("group"), lax.axis_size("head")
+    group_index, head_index = lax.axis_index("group"), lax.axis_index("head")
+    width = attended.shape[1]
+    mixed = jnp.zeros((tok_rows, groups * part_cols), jnp.bfloat16)
+    for dg in range(groups):
+        total = None
+        for dh in range(heads):
+            piece = attended
+            if dg or dh:
+                pairs = [
+                    (a * heads + b, (a + dg) % groups * heads + (b + dh) % heads)
+                    for a in range(groups)
+                    for b in range(heads)
+                ]
+                piece = lax.ppermute(attended, ("group", "head"), pairs)
+            source = lax.rem(head_index - dh + heads, heads)
+            rows = lax.dynamic_slice_in_dim(weight_part, source * width, width, 0)
+            product = jnp.dot(piece, rows, preferred_element_type=jnp.float32)
+            total = product if total is None else total + product
+        share = total.astype(jnp.bfloat16)
+        if dg:
+            share = lax.ppermute(share, "group", [(a, (a - dg) % groups) for a in range(groups)])
+        column = lax.rem(group_index + dg, groups) * part_cols
+        mixed = lax.dynamic_update_slice(mixed, share, (0, column))
+    return mixed
 
 
 def solution(mesh):

time: 353 us -> 243 us (0.69)
  waiting for transfers between devices: 253 us -> 150 us
  matrix products: 47.3 us -> 29.4 us
  local copies, waits for them, and re-layouts: 7.46 us -> 16.4 us
  starting transfers between devices: 22 us -> 25.6 us
    all_gather x2 -> x1, waiting for transfers between devices: 239 us -> 0.01 us  [per_device(): weight_part = lax.all_gather(weight_part, 'ctx', axis=0, tiled=True)]
    ppermute x8, waiting for transfers between devices: 13.3 us -> 99.4 us  [passed_along(): return lax.ppermute(array, axis, pairs)]
    ppermute x0 -> x4, waiting for transfers between devices: none -> 50.8 us  [the longest x3 41.9 us: per_device(): piece = lax.ppermute(attended, ('group', 'head'), pairs)]
    dot_general x5, matrix products: 24.5 us -> 7.08 us  [update(): jnp.einsum('hgqk,khd->hgqd', weights.astype(jnp.bfloat16), value_head_row...]
    ppermute x0 -> x4, starting transfers between devices: none -> 8.59 us  [the longest x3 8.39 us: per_device(): piece = lax.ppermute(attended, ('group', 'head'), pairs)]
    ppermute x4, local copies, waits for them, and re-layouts: 1.7 us -> 7.18 us  [passed_along(): return lax.ppermute(array, axis, pairs)]
    ppermute x8, starting transfers between devices: 21.9 us -> 17.1 us  [passed_along(): return lax.ppermute(array, axis, pairs)]
    dot_general x1 -> x4, matrix products: 11.9 us -> 11.5 us  [per_device(): product = jnp.dot(piece, rows, preferred_element_type=jnp.float32)]
  transfers between devices with their start and end apart: 10 -> 13, of which waited for: 4 -> 9; matrix products, arithmetic and copies ran while one was open for 12% -> 20% of each run, Pallas kernels for 0% -> 0%
where the time goes in v1:
time: 243 us; the launch traced here: 242 us
  waiting for transfers between devices  150 us (62%)
  matrix products  29.4 us (12%)
  starting transfers between devices  25.6 us (11%)
  local copies, waits for them, and re-layouts  16.4 us (7%)
  between operations  13.8 us (6%)
  other arithmetic  6.66 us (3%)
    ppermute x8, waiting for transfers between devices, passed_along(): return lax.ppermute(array, axis, pairs)  99.4 us
    ppermute x3, waiting for transfers between devices, per_device(): piece = lax.ppermute(attended, ('group', 'head'), pairs)  41.9 us
    ppermute x8, starting transfers between devices, passed_along(): return lax.ppermute(array, axis, pairs)  17.1 us
    dot_general x4, matrix products, per_device(): product = jnp.dot(piece, rows, preferred_element_type=jnp.float32)  11.5 us
    dot_general x5, matrix products, update(): jnp.einsum('qhgd,khd->hgqk', query_head_rows, key_head_rows, preferred_el...  10.8 us
    ppermute x1, waiting for transfers between devices, per_device(): lax.ppermute(share, 'group', [(a, (a - dg) % groups) for a in range(group...  8.88 us
    ppermute x3, starting transfers between devices, per_device(): piece = lax.ppermute(attended, ('group', 'head'), pairs)  8.39 us
    ppermute x4, local copies, waits for them, and re-layouts, passed_along(): return lax.ppermute(array, axis, pairs)  7.18 us
  transfers between devices with their start and end apart: 13, of which 9 were waited for; matrix products, arithmetic and copies ran while one was open for 20% of the time, Pallas kernels for 0%

profile of v1, /device:TPU:17, one launch (start us, length us, event | category | flops | bytes accessed | tf_op | source)
XLA Modules:
  0.0 242.1 jit_solution(17896952337033381033)
XLA Ops:
  6.6 1.6 copy-done
  8.1 1.1 constant_dynamic-slice_fusion
  9.2 3.1 %collective-permute-start.1 = (bf16[256,512]{1,0:T(8,128)(2,1)}, bf16[256,512]{1,0:T(8,128)(2,1)}, u32[]{:S(2)}, u32[]{:S(2)}) collective-permute-start(bf16[256,512]{1,0:T(8,128)(2,1)} %param.7), channel_id=1, source_target_pairs={{0,2},{2,4},{4,6},{6,8},{8,10},{10,12},{12,14},{1,3},{3,5},{5,7},{... | collective-permute-start | bytes 786440 | tf_op jit(solution)/shard_map/ppermute | solution.py:15
  12.3 3.2 %collective-permute-start.3 = (bf16[256,512]{1,0:T(8,128)(2,1)}, bf16[256,512]{1,0:T(8,128)(2,1)}, u32[]{:S(2)}, u32[]{:S(2)}) collective-permute-start(bf16[256,512]{1,0:T(8,128)(2,1)} %param.7), channel_id=1, source_target_pairs={{0,4},{2,6},{4,8},{6,10},{8,12},{10,14},{1,5},{3,7},{5,9},{7,11},{... | collective-permute-start | bytes 786440 | tf_op jit(solution)/shard_map/ppermute | solution.py:15
  15.6 1.9 collective-permute-start.5
  17.5 1.3 collective-permute-start.7
  18.8 1.8 copy.50
  20.6 1.3 collective-permute-start.6
  21.9 1.0 reshape.264
  23.0 0.9 copy.87
  23.8 1.8 reshape.265
  25.8 1.2 compare_and_fusion.4
  27.0 2.9 %fusion = (f32[4,4,256]{2,1,0:T(4,128)S(1)}, f32[4,256,256,4]{2,1,3,0:T(8,128)}) fusion(pred[256,256]{0,1:T(8,128)(4,1)S(1)} %get-tuple-element.21, bf16[256,4,4,128]{3,2,1,0:T(4,128)(2,1)S(1)} %reshape.265, bf16[256,4,128,1]{2,1,0,3:T(4,128)(2,1)S(1)} %bitcast.243), kind=kOutput, calls=%fused_computation.10 | convolution fusion | flops 271577088 | bytes 5586944 | tf_op jit(solution)/shard_map/qhgd,khd->hgqk/dot_general | solution.py:33
  29.9 1.9 collective-permute-start.4
  31.8 1.8 copy.53
  33.6 1.9 collective-permute-start.2
  35.5 1.8 copy.58
  37.3 1.3 collective-permute-done.5
  38.6 2.4 collective-permute-start
  41.0 1.8 copy.63
  42.8 1.1 collective-permute-done.7
  43.9 1.8 copy.68
  45.7 9.4 %collective-permute-done.6 = bf16[256,512]{0,1:T(8,128)(2,1)} collective-permute-done((bf16[256,512]{0,1:T(8,128)(2,1)}, bf16[256,512]{0,1:T(8,128)(2,1)}, u32[]{:S(2)}, u32[]{:S(2)}) %collective-permute-start.6) | collective-permute-done | bytes 262176 | tf_op jit(solution)/shard_map/ppermute | solution.py:15
  55.1 2.0 fusion.4
  57.1 15.2 %collective-permute-done.4 = bf16[256,512]{0,1:T(8,128)(2,1)} collective-permute-done((bf16[256,512]{0,1:T(8,128)(2,1)}, bf16[256,512]{0,1:T(8,128)(2,1)}, u32[]{:S(2)}, u32[]{:S(2)}) %collective-permute-start.4) | collective-permute-done | bytes 262176 | tf_op jit(solution)/shard_map/ppermute | solution.py:15
  72.3 2.0 fusion.3
  74.3 20.1 %collective-permute-done.2 = bf16[256,512]{0,1:T(8,128)(2,1)} collective-permute-done((bf16[256,512]{0,1:T(8,128)(2,1)}, bf16[256,512]{0,1:T(8,128)(2,1)}, u32[]{:S(2)}, u32[]{:S(2)}) %collective-permute-start.2) | collective-permute-done | bytes 262176 | tf_op jit(solution)/shard_map/ppermute | solution.py:15
  94.5 2.0 fusion.2
  96.4 52.3 %collective-permute-done = bf16[256,512]{0,1:T(8,128)(2,1)} collective-permute-done((bf16[256,512]{0,1:T(8,128)(2,1)}, bf16[256,512]{0,1:T(8,128)(2,1)}, u32[]{:S(2)}, u32[]{:S(2)}) %collective-permute-start) | collective-permute-done | bytes 262176 | tf_op jit(solution)/shard_map/ppermute | solution.py:15
  148.7 2.0 fusion.1
  150.7 1.1 fusion.15
  151.7 1.1 fusion.17
  152.8 1.0 fusion.19
  153.9 1.1 fusion.21
  155.0 1.1 fusion.13
  156.1 1.2 fusion.31
  157.4 1.2 fusion.29
  158.7 1.5 fusion.27
  160.1 1.2 fusion.25
  161.4 1.9 fusion.34
  163.3 7.9 %collective-permute-start.10 = (bf16[256,2048]{0,1:T(8,128)(2,1)S(1)}, bf16[256,2048]{0,1:T(8,128)(2,1)}, u32[]{:S(2)}, u32[]{:S(2)}) collective-permute-start(bf16[256,2048]{0,1:T(8,128)(2,1)S(1)} %bitcast.251), channel_id=1, source_target_pairs={{0,17},{1,16},{16,1},{17,0},{2,19},{3,18},{18,3},{19,2},{4,21},{5,... | collective-permute-start | bytes 3145736 | tf_op jit(solution)/shard_map/ppermute | solution.py:117
  171.7 23.4 %collective-permute-done.10 = bf16[256,2048]{0,1:T(8,128)(2,1)} collective-permute-done((bf16[256,2048]{0,1:T(8,128)(2,1)S(1)}, bf16[256,2048]{0,1:T(8,128)(2,1)}, u32[]{:S(2)}, u32[]{:S(2)}) %collective-permute-start.10) | collective-permute-done | bytes 1048608 | tf_op jit(solution)/shard_map/ppermute | solution.py:117
  195.1 3.9 %fusion.5 = f32[256,1024]{1,0:T(8,128)S(1)} fusion(bf16[256,2048]{0,1:T(8,128)(2,1)} %collective-permute-done.10, bf16[4096,1024]{1,0:T(8,128)(2,1)} %all-gather.2.cloned.1.call-done, s32[]{:T(128)S(6)} %select_n.125), kind=kOutput, calls=%fused_computation.15 | convolution fusion | flops 1073741824 | bytes 6291460 | tf_op jit(solution)/shard_map/dot_general | solution.py:120
  199.0 18.5 %collective-permute-done.9 = bf16[256,2048]{0,1:T(8,128)(2,1)} collective-permute-done((bf16[256,2048]{0,1:T(8,128)(2,1)S(1)}, bf16[256,2048]{0,1:T(8,128)(2,1)}, u32[]{:S(2)}, u32[]{:S(2)}) %collective-permute-start.9) | collective-permute-done | bytes 1048608 | tf_op jit(solution)/shard_map/ppermute | solution.py:117
  217.6 3.8 %fusion.76 = bf16[256,1024]{1,0:T(8,128)(2,1)S(1)} fusion(f32[256,1024]{1,0:T(8,128)S(1)} %fusion.5, bf16[256,2048]{0,1:T(8,128)(2,1)} %collective-permute-done.9, bf16[4096,1024]{1,0:T(8,128)(2,1)} %all-gather.2.cloned.1.call-done, s32[]{:T(128)S(6)} %select_n.124), kind=kOutput, calls=%fused_computation.78 | convolution fusion | flops 1074266112 | bytes 6815748 | tf_op jit(solution)/shard_map/dot_general | solution.py:120
  221.6 1.3 fusion.11
  223.0 2.5 %fusion.73 = bf16[256,2048]{1,0:T(8,128)(2,1)S(1)} fusion(bf16[256,2048]{1,0:T(8,128)(2,1)S(1)} %broadcast_in_dim.129, s32[]{:T(128)S(6)} %select_n.126, f32[256,1024]{1,0:T(8,128)S(1)} %fusion.11, bf16[256,2048]{0,1:T(8,128)(2,1)} %collective-permute-done.8, bf16[4096,1024]{1,0:T(8,128)(2,1)S(1)} %bitcast.250, s32[]{:T(128)S(6)} %select_n.125), kind=kOutput, calls=%fused_computation.77 | convolution fusion | flops 1074266112 | bytes 6815752 | tf_op jit(solution)/shard_map/dot_general | solution.py:120
  225.5 8.9 %collective-permute-done.11 = bf16[256,1024]{1,0:T(8,128)(2,1)S(1)} collective-permute-done((bf16[256,1024]{1,0:T(8,128)(2,1)S(1)}, bf16[256,1024]{1,0:T(8,128)(2,1)S(1)}, u32[]{:S(2)}, u32[]{:S(2)}) %collective-permute-start.11) | collective-permute-done | bytes 524320 | tf_op jit(solution)/shard_map/ppermute | solution.py:124
  (51 shorter events, 2.0 us)
Async XLA Ops:
  6.5 1.6 copy-start
  6.5 16.4 %copy-start.7 = (bf16[256,512]{1,0:T(8,128)(2,1)S(1)}, bf16[256,512]{1,0:T(8,128)(2,1)}, u32[]{:S(2)}) copy-start(bf16[256,512]{1,0:T(8,128)(2,1)} %param.7) | copy-start | bytes 786436
  6.5 19.1 %copy-start.13 = (s32[16]{0:T(128)S(1)}, s32[16]{0:T(128)}, u32[]{:S(2)}) copy-start(s32[16]{0:T(128)} %param.8) | copy-start | bytes 196
  6.5 188.6 %all-gather.2.cloned.1.call-start = ((), (), s32[]{:S(2)}) async-start(), calls=%async_computation | async-start | bytes 9437184 | tf_op jit(solution)/shard_map/all_gather | solution.py:83
  9.2 20.6 %collective-permute-start.1 = (bf16[256,512]{1,0:T(8,128)(2,1)}, bf16[256,512]{1,0:T(8,128)(2,1)}, u32[]{:S(2)}, u32[]{:S(2)}) collective-permute-start(bf16[256,512]{1,0:T(8,128)(2,1)} %param.7), channel_id=1, source_target_pairs={{0,2},{2,4},{4,6},{6,8},{8,10},{10,12},{12,14},{1,3},{3,5},{5,7},{... | collective-permute-start | bytes 786440 | tf_op jit(solution)/shard_map/ppermute | solution.py:15
  12.3 21.2 %collective-permute-start.3 = (bf16[256,512]{1,0:T(8,128)(2,1)}, bf16[256,512]{1,0:T(8,128)(2,1)}, u32[]{:S(2)}, u32[]{:S(2)}) collective-permute-start(bf16[256,512]{1,0:T(8,128)(2,1)} %param.7), channel_id=1, source_target_pairs={{0,4},{2,6},{4,8},{6,10},{8,12},{10,14},{1,5},{3,7},{5,9},{7,11},{... | collective-permute-start | bytes 786440 | tf_op jit(solution)/shard_map/ppermute | solution.py:15
  15.6 23.0 %collective-permute-start.5 = (bf16[256,512]{1,0:T(8,128)(2,1)}, bf16[256,512]{1,0:T(8,128)(2,1)}, u32[]{:S(2)}, u32[]{:S(2)}) collective-permute-start(bf16[256,512]{1,0:T(8,128)(2,1)} %param.7), channel_id=1, source_target_pairs={{0,6},{2,8},{4,10},{6,12},{8,14},{1,7},{3,9},{5,11},{7,13},{9,15},... | collective-permute-start | bytes 786440 | tf_op jit(solution)/shard_map/ppermute | solution.py:15
  17.5 26.4 %collective-permute-start.7 = (bf16[256,512]{1,0:T(8,128)(2,1)}, bf16[256,512]{1,0:T(8,128)(2,1)}, u32[]{:S(2)}, u32[]{:S(2)}) collective-permute-start(bf16[256,512]{1,0:T(8,128)(2,1)} %param.7), channel_id=1, source_target_pairs={{0,8},{2,10},{4,12},{6,14},{1,9},{3,11},{5,13},{7,15},{16,24},{18,... | collective-permute-start | bytes 786440 | tf_op jit(solution)/shard_map/ppermute | solution.py:15
  20.6 34.5 %collective-permute-start.6 = (bf16[256,512]{0,1:T(8,128)(2,1)}, bf16[256,512]{0,1:T(8,128)(2,1)}, u32[]{:S(2)}, u32[]{:S(2)}) collective-permute-start(bf16[256,512]{0,1:T(8,128)(2,1)} %copy.50), channel_id=1, source_target_pairs={{0,8},{2,10},{4,12},{6,14},{1,9},{3,11},{5,13},{7,15},{16,24},{18,... | collective-permute-start | bytes 786440 | tf_op jit(solution)/shard_map/ppermute | solution.py:15
  27.0 2.9 %copy-start.5 = (pred[256,256]{0,1:T(8,128)(4,1)}, pred[256,256]{0,1:T(8,128)(4,1)S(1)}, u32[]{:S(2)}) copy-start(pred[256,256]{0,1:T(8,128)(4,1)S(1)} %get-tuple-element.21) | copy-start | bytes 196612
  29.9 42.4 %collective-permute-start.4 = (bf16[256,512]{0,1:T(8,128)(2,1)}, bf16[256,512]{0,1:T(8,128)(2,1)}, u32[]{:S(2)}, u32[]{:S(2)}) collective-permute-start(bf16[256,512]{0,1:T(8,128)(2,1)} %copy.50), channel_id=1, source_target_pairs={{0,6},{2,8},{4,10},{6,12},{8,14},{1,7},{3,9},{5,11},{7,13},{9,15},... | collective-permute-start | bytes 786440 | tf_op jit(solution)/shard_map/ppermute | solution.py:15
  33.6 60.9 %collective-permute-start.2 = (bf16[256,512]{0,1:T(8,128)(2,1)}, bf16[256,512]{0,1:T(8,128)(2,1)}, u32[]{:S(2)}, u32[]{:S(2)}) collective-permute-start(bf16[256,512]{0,1:T(8,128)(2,1)} %copy.50), channel_id=1, source_target_pairs={{0,4},{2,6},{4,8},{6,10},{8,12},{10,14},{1,5},{3,7},{5,9},{7,11},{... | collective-permute-start | bytes 786440 | tf_op jit(solution)/shard_map/ppermute | solution.py:15
  38.6 110.1 %collective-permute-start = (bf16[256,512]{0,1:T(8,128)(2,1)}, bf16[256,512]{0,1:T(8,128)(2,1)}, u32[]{:S(2)}, u32[]{:S(2)}) collective-permute-start(bf16[256,512]{0,1:T(8,128)(2,1)} %copy.50), channel_id=1, source_target_pairs={{0,2},{2,4},{4,6},{6,8},{8,10},{10,12},{12,14},{1,3},{3,5},{5,7},{... | collective-permute-start | bytes 786440 | tf_op jit(solution)/shard_map/ppermute | solution.py:15
  55.1 39.3 %copy-start.3 = (pred[256,256]{0,1:T(8,128)(4,1)S(1)}, pred[256,256]{0,1:T(8,128)(4,1)}, u32[]{:S(2)}) copy-start(pred[256,256]{0,1:T(8,128)(4,1)} %get-tuple-element.24) | copy-start | bytes 196612
  72.3 76.4 %copy-start.4 = (pred[256,256]{0,1:T(8,128)(4,1)S(1)}, pred[256,256]{0,1:T(8,128)(4,1)}, u32[]{:S(2)}) copy-start(pred[256,256]{0,1:T(8,128)(4,1)} %get-tuple-element.22) | copy-start | bytes 196612
  152.8 2.2 copy-start.1
  152.8 2.2 copy-start.6
  153.9 2.3 copy-start.8
  156.1 1.3 copy-start.9
  157.4 1.3 copy-start.10
  158.6 1.5 copy-start.12
  160.1 1.2 copy-start.11
  163.3 31.8 %collective-permute-start.10 = (bf16[256,2048]{0,1:T(8,128)(2,1)S(1)}, bf16[256,2048]{0,1:T(8,128)(2,1)}, u32[]{:S(2)}, u32[]{:S(2)}) collective-permute-start(bf16[256,2048]{0,1:T(8,128)(2,1)S(1)} %bitcast.251), channel_id=1, source_target_pairs={{0,17},{1,16},{16,1},{17,0},{2,19},{3,18},{18,3},{19,2},{4,21},{5,... | collective-permute-start | bytes 3145736 | tf_op jit(solution)/shard_map/ppermute | solution.py:117
  171.2 46.3 %collective-permute-start.9 = (bf16[256,2048]{0,1:T(8,128)(2,1)S(1)}, bf16[256,2048]{0,1:T(8,128)(2,1)}, u32[]{:S(2)}, u32[]{:S(2)}) collective-permute-start(bf16[256,2048]{0,1:T(8,128)(2,1)S(1)} %bitcast.252), channel_id=1, source_target_pairs={{0,16},{1,17},{16,0},{17,1},{2,18},{3,19},{18,2},{19,3},{4,20},{5,... | collective-permute-start | bytes 3145736 | tf_op jit(solution)/shard_map/ppermute | solution.py:117
  171.4 51.4 %collective-permute-start.8 = (bf16[256,2048]{0,1:T(8,128)(2,1)S(1)}, bf16[256,2048]{0,1:T(8,128)(2,1)}, u32[]{:S(2)}, u32[]{:S(2)}) collective-permute-start(bf16[256,2048]{0,1:T(8,128)(2,1)S(1)} %bitcast.253), channel_id=1, source_target_pairs={{0,1},{1,0},{16,17},{17,16},{2,3},{3,2},{18,19},{19,18},{4,5},{5,4... | collective-permute-start | bytes 3145736 | tf_op jit(solution)/shard_map/ppermute | solution.py:117
  195.1 26.5 %slice-start = ((s8[8388608]{0:T(1024)(128)(4,1)}), s8[4194304]{0:T(1024)(128)(4,1)S(1)}, s32[]{:S(2)}) async-start(s8[8388608]{0:T(1024)(128)(4,1)} %bitcast.249), calls=%async_computation.1 | async-start | bytes 8388608
  199.0 22.5 %slice-start.1 = ((s8[8388608]{0:T(1024)(128)(4,1)}), s8[4194304]{0:T(1024)(128)(4,1)S(1)}, s32[]{:S(2)}) async-start(s8[8388608]{0:T(1024)(128)(4,1)} %bitcast.249), calls=%async_computation.2 | async-start | bytes 8388608
  221.4 13.0 %collective-permute-start.11 = (bf16[256,1024]{1,0:T(8,128)(2,1)S(1)}, bf16[256,1024]{1,0:T(8,128)(2,1)S(1)}, u32[]{:S(2)}, u32[]{:S(2)}) collective-permute-start(bf16[256,1024]{1,0:T(8,128)(2,1)S(1)} %fusion.76), channel_id=1, source_target_pairs={{0,16},{16,0},{1,17},{17,1},{2,18},{18,2},{3,19},{19,3},{4,20},{20... | collective-permute-start | bytes 1572872 | tf_op jit(solution)/shard_map/ppermute | solution.py:124
  225.5 8.9 %copy-start.2 = (bf16[256,2048]{1,0:T(8,128)(2,1)}, bf16[256,2048]{1,0:T(8,128)(2,1)S(1)}, u32[]{:S(2)}) copy-start(bf16[256,2048]{1,0:T(8,128)(2,1)S(1)} %fusion.73) | copy-start | bytes 3145732
Sparse Core Ops, SparseCore 0:
  9.5 168.5 all-gather.1

commit v2 on v0

v2 whole, which is shorter than its diff:
```python
import functools
import math

import jax
import jax.numpy as jnp
from jax import lax
from jax.experimental import pallas as pl
from jax.experimental.pallas import tpu as pltpu
from jax.sharding import PartitionSpec as P

HEAD_SIZE = 128
BLOCK_TOKENS = 128
MESH = pl.DeviceIdType.MESH


def fused(
    groups, ctx_count, heads, reach,
    q_ref, k_ref, v_ref, bias_ref, w_ref, out_ref,
    kv, wbuf, abuf, cbuf, crecv, local_sem,
    line_send, line_recv, mate_send, mate_recv,
    wmate_send, wmate_recv, wline_send, wline_recv,
    plane_send, plane_recv, core_send, core_recv, c_send, c_recv,
):
    g, c, h = lax.axis_index("group"), lax.axis_index("ctx"), lax.axis_index("head")
    x, z = lax.rem(c, 2), c // 2
    lines, steps = ctx_count // 2, reach // 2
    tok = q_ref.shape[0]
    kv_heads = k_ref.shape[1] // HEAD_SIZE
    group_width = q_ref.shape[1] // k_ref.shape[1]
    chunk = group_width * HEAD_SIZE
    shard = w_ref.shape[0]
    part = wbuf.shape[1]
    parts = 2 * groups
    me = g * 2 + x
    mate = c + 1 - 2 * x
    offsets = [(dg, dx) for dg in range(groups) for dx in range(2) if dg or dx]

    def copy(src, dst, send, recv, device):
        return pltpu.make_async_remote_copy(
            src_ref=src, dst_ref=dst, send_sem=send, recv_sem=recv,
            device_id=device, device_id_type=MESH,
        )

    def guarded(condition, action):
        if condition is None:
            action()
        else:
            pl.when(condition)(action)

    barrier = pltpu.get_barrier_semaphore()

    def greet(device):
        pl.semaphore_signal(barrier, inc=1, device_id=device, device_id_type=MESH)

    def plane_to(dg, dx):
        return (lax.rem(g + dg, groups), 2 * z + lax.rem(x + dx, 2), h)

    def plane_from(dg, dx):
        return lax.rem(g - dg + groups, groups) * 2 + lax.rem(x + dx, 2)

    for dg, dx in offsets:
        greet(plane_to(dg, dx))
    for dh in range(1, heads):
        greet((g, c, lax.rem(h + dh, heads)))
    up, down = z + 1 < lines, z >= 1
    pl.when(up)(lambda: greet((g, c + 2, h)))
    pl.when(down)(lambda: greet((g, c - 2, h)))
    pl.semaphore_wait(
        barrier, len(offsets) + heads - 1 + up.astype(jnp.int32) + down.astype(jnp.int32)
    )

    pending = []

    def start(condition, make):
        guarded(condition, lambda: make().start())
        pending.append((condition, make))

    def received(condition, make):
        guarded(condition, lambda: make().wait_recv())

    kv[0, 0] = k_ref[...]
    kv[0, 1] = v_ref[...]

    def line_copy(s):
        return lambda: copy(
            kv.at[2 * (s - 1)], kv.at[2 * s], line_send.at[s - 1], line_recv.at[s - 1], (g, c + 2, h)
        )

    def mate_copy(m, side):
        return lambda: copy(
            kv.at[2 * m + 2 * side], kv.at[2 * m + 1], mate_send.at[m], mate_recv.at[m], (g, mate, h)
        )

    start(up, line_copy(1))
    start(x == 0, mate_copy(0, 0))

    def rows_of(source):
        return pl.ds(pl.multiple_of(source * shard, shard), shard)

    def columns_of(which):
        return pl.ds(pl.multiple_of(which * part, part), part)

    own = pltpu.make_async_copy(w_ref.at[:, columns_of(me)], wbuf.at[rows_of(c)], local_sem)
    own.start()

    def wmate_copy():
        return copy(
            w_ref.at[:, columns_of(g * 2 + 1 - x)], wbuf.at[rows_of(c)],
            wmate_send, wmate_recv, (g, mate, h),
        )

    start(None, wmate_copy)

    def wline_copy(way, s, which):
        def make():
            line = z - s if way == 0 else z + s
            source = 2 * line + (x if which == 0 else 1 - x)
            rows = rows_of(source)
            to = c + 2 if way == 0 else c - 2
            return copy(
                wbuf.at[rows], wbuf.at[rows],
                wline_send.at[way, s, which], wline_recv.at[way, s, which], (g, to, h),
            )
        return make

    def wline_sends(way, s):
        if way == 0:
            return up & (z >= s)
        return down & (z + s < lines)

    def wline_arrives(way, s):
        return z >= s + 1 if way == 0 else z + s + 1 < lines

    def pump_weights(s):
        for which in range(2):
            for way in range(2):
                received(wline_arrives(way, s), wline_copy(way, s, which))
                if s + 1 < lines - 1:
                    start(wline_sends(way, s + 1), wline_copy(way, s + 1, which))

    own.wait()
    for way in (1, 0):
        start(wline_sends(way, 0), wline_copy(way, 0, 0))

    for s in range(1, steps + 1):
        received(z >= s, line_copy(s))
        if s < steps:
            start(up & (z >= s), line_copy(s + 1))
            start((x == 0) & (z >= s), mate_copy(s, 0))
        start((x == 1) & (z >= s), mate_copy(s - 1, 1))
    received(None, wmate_copy)
    for way in (1, 0):
        start(wline_sends(way, 0), wline_copy(way, 0, 1))
    for m in range(steps):
        received(c >= 2 * m + 1, mate_copy(m, 0))
    for d in range(1, reach + 1):

        @pl.when(c < d)
        def _():
            kv[d] = jnp.zeros(kv.shape[1:], kv.dtype)

    scale = math.log2(math.e) / math.sqrt(HEAD_SIZE)

    def slot(d, which, column):
        rows = pl.ds(0, tok) if d < reach else pl.ds(tok - BLOCK_TOKENS, BLOCK_TOKENS)
        return kv[d, which, rows, column]

    def plane_copy(hk, i):
        def make():
            j = h * kv_heads + hk
            return copy(
                abuf.at[me, j], abuf.at[me, j],
                plane_send.at[i, hk], plane_recv.at[i, hk], plane_to(*offsets[i]),
            )
        return make

    def core_copy(hk, i, dh):
        def make():
            p = me if i == len(offsets) else plane_from(*offsets[i])
            j = h * kv_heads + hk
            return copy(
                abuf.at[p, j], abuf.at[p, j],
                core_send.at[i, hk, dh - 1], core_recv.at[i, hk, dh - 1],
                (g, c, lax.rem(h + dh, heads)),
            )
        return make

    def relay(hk):
        for i in range(len(offsets)):
            received(None, plane_copy(hk, i))
            for dh in range(1, heads):
                start(None, core_copy(hk, i, dh))

    pumped = 0
    for hk in range(kv_heads):
        column = pl.ds(hk * HEAD_SIZE, HEAD_SIZE)

        @pl.loop(0, group_width)
        def _(n):
            at = pl.multiple_of(hk * chunk + n * HEAD_SIZE, HEAD_SIZE)
            query = q_ref[:, pl.ds(at, HEAD_SIZE)]
            scores, top = [], None
            for d in range(reach + 1):
                keys = slot(d, 0, column)
                s = lax.dot_general(
                    query, keys, (((1,), (1,)), ((), ())), preferred_element_type=jnp.float32
                )
                s = s + bias_ref[:, pl.ds(d * tok, keys.shape[0])]
                scores.append(s)
                high = jnp.max(s, axis=-1, keepdims=True)
                top = high if top is None else jnp.maximum(top, high)
            total, summed = None, None
            for d in range(reach + 1):
                weights = jnp.exp2((scores[d] - top) * scale)
                t = jnp.sum(weights, axis=-1, keepdims=True)
                o = jnp.dot(
                    weights.astype(jnp.bfloat16), slot(d, 1, column),
                    preferred_element_type=jnp.float32,
                )
                total = t if total is None else total + t
                summed = o if summed is None else summed + o
            to = pl.multiple_of(n * HEAD_SIZE, HEAD_SIZE)
            abuf[me, h * kv_heads + hk, :, pl.ds(to, HEAD_SIZE)] = (summed / total).astype(
                jnp.bfloat16
            )

        for i in reversed(range(len(offsets))):
            start(None, plane_copy(hk, i))
        for dh in range(1, heads):
            start(None, core_copy(hk, len(offsets), dh))
        if hk % 2 == 0 and pumped < lines - 2:
            pump_weights(pumped)
            pumped += 1
        if hk >= 2:
            relay(hk - 2)
    for hk in range(max(kv_heads - 2, 0), kv_heads):
        relay(hk)
    while pumped < lines - 1:
        pump_weights(pumped)
        pumped += 1
    for hk in range(kv_heads):
        for i in range(len(offsets) + 1):
            for dh in range(1, heads):
                received(None, core_copy(hk, i, dh))

    def c_copy(i):
        def make():
            dg, dx = offsets[i]
            return copy(cbuf.at[i], crecv.at[me], c_send.at[i], c_recv.at[i], plane_to(dg, dx))
        return make

    def project(p):
        total = None
        for j in range(heads * kv_heads):
            product = jnp.dot(
                abuf[p, j], wbuf[j * chunk:(j + 1) * chunk, :], preferred_element_type=jnp.float32
            )
            total = product if total is None else total + product
        return total.astype(jnp.bfloat16)

    for i in reversed(range(len(offsets))):
        dg, dx = offsets[i]
        cbuf[i] = project(lax.rem(g + dg, groups) * 2 + lax.rem(x + dx, 2))
        start(None, c_copy(i))
    out_ref[:, columns_of(me)] = project(me)
    for i in reversed(range(len(offsets))):
        received(None, c_copy(i))
        source = plane_from(*offsets[i])
        out_ref[:, columns_of(source)] = crecv[source]
    for condition, make in pending:
        guarded(condition, lambda make=make: make().wait_send())


def per_device(queries, keys, values, doc_of_block, out_weight):
    tok = queries.shape[0]
    kv_heads = keys.shape[1] // HEAD_SIZE
    groups, ctx_count, heads = (lax.axis_size(a) for a in ("group", "ctx", "head"))
    reach = min(8, ctx_count // 2)
    lines, steps = ctx_count // 2, reach // 2
    parts = 2 * groups
    part = out_weight.shape[1] // parts
    chunk = queries.shape[1] // kv_heads
    start = lax.axis_index("ctx") * tok
    query_pos = start + jnp.arange(tok, dtype=jnp.int32)
    key_pos = jnp.concatenate(
        [
            start - d * tok + jnp.arange(0 if d < reach else tok - BLOCK_TOKENS, tok, dtype=jnp.int32)
            for d in range(reach + 1)
        ]
    )
    table = jnp.arange(doc_of_block.shape[0], dtype=jnp.int32)

    def docs(positions):
        matches = jnp.floor_divide(positions, BLOCK_TOKENS)[:, None] == table[None, :]
        return jnp.max(jnp.where(matches, doc_of_block[None, :], -1), axis=1)

    visible = (docs(key_pos)[None, :] == docs(query_pos)[:, None]) & (
        key_pos[None, :] <= query_pos[:, None]
    )
    bias = jnp.where(visible, 0.0, -1e30).astype(jnp.float32)
    dma = pltpu.SemaphoreType.DMA
    bf16 = jnp.bfloat16
    vmem = pl.BlockSpec(memory_space=pltpu.VMEM)
    return pl.pallas_call(
        functools.partial(fused, groups, ctx_count, heads, reach),
        out_shape=jax.ShapeDtypeStruct((tok, out_weight.shape[1]), bf16),
        in_specs=[vmem, vmem, vmem, vmem, pl.BlockSpec(memory_space=pl.ANY)],
        out_specs=vmem,
        scratch_shapes=[
            pltpu.VMEM((reach + 1, 2, tok, keys.shape[1]), bf16),
            pltpu.VMEM((ctx_count * out_weight.shape[0], part), bf16),
            pltpu.VMEM((parts, heads * kv_heads, tok, chunk), bf16),
            pltpu.VMEM((parts - 1, tok, part), bf16),
            pltpu.VMEM((parts, tok, part), bf16),
            dma,
            dma((steps,)), dma((steps,)), dma((steps,)), dma((steps,)),
            dma, dma,
            dma((2, lines - 1, 2)), dma((2, lines - 1, 2)),
            dma((parts - 1, kv_heads)), dma((parts - 1, kv_heads)),
            dma((parts, kv_heads, heads - 1)), dma((parts, kv_heads, heads - 1)),
            dma((parts - 1,)), dma((parts - 1,)),
        ],
        compiler_params=pltpu.CompilerParams(
            collective_id=0, has_side_effects=True, vmem_limit_bytes=48 * 1024 * 1024
        ),
    )(queries, keys, values, bias, out_weight)


def solution(mesh):
    return jax.shard_map(
        per_device,
        mesh=mesh,
        in_specs=(
            P(("group", "ctx"), "head"),
            P(("group", "ctx"), "head"),
            P(("group", "ctx"), "head"),
            P("group"),
            P("ctx", "head"),
        ),
        out_specs=P(("group", "ctx"), "head"),
        check_vma=False,
    )
```

time: 353 us -> 120 us (0.34)
  waiting for transfers between devices: 253 us -> 0 us
  Pallas kernels: 0 us -> 112 us
  matrix products: 47.3 us -> 0 us
  starting transfers between devices: 22 us -> 0 us
  between operations: 13.7 us -> 0.08 us
  other arithmetic: 6.66 us -> 1.86 us
    all_gather x2 -> x0, waiting for transfers between devices: 239 us -> none  [the longest x1 229 us: per_device(): lax.all_gather(out_weight, 'ctx', axis=0, tiled=True)]
    pallas_call x0 -> x1, Pallas kernels: none -> 112 us  [per_device(): pl.pallas_call(functools.partial(fused, groups, ctx_count, heads, reach),...]
    dot_general x11 -> x0, matrix products: 47.3 us -> none  [the longest x5 24.5 us: update(): jnp.einsum('hgqk,khd->hgqd', weights.astype(jnp.bfloat16), value_head_row...]
    ppermute x8 -> x0, starting transfers between devices: 21.9 us -> none  [passed_along(): return lax.ppermute(array, axis, pairs)]
    ppermute x8 -> x0, waiting for transfers between devices: 13.3 us -> none  [passed_along(): return lax.ppermute(array, axis, pairs)]
    reduce_sum x5 -> x0, other arithmetic: 5.24 us -> none  [update(): totals = totals * rescale + jnp.sum(weights, axis=-1)]
    reshape x3 -> x0, local copies, waits for them, and re-layouts: 4.66 us -> none  [the longest x1 1.85 us: update(): value_head_rows = value_piece.reshape(rows_here, kv_heads, HEAD_SIZE)]
  transfers between devices with their start and end apart: 10 -> 0, of which waited for: 4 -> 0; matrix products, arithmetic and copies ran while one was open for 12% -> 0% of each run, Pallas kernels for 0% -> 0%
where the time goes in v2:
time: 120 us; the launch traced here: 118 us
  Pallas kernels  112 us (93%)
  local copies, waits for them, and re-layouts  4.46 us (4%)
  other arithmetic  1.86 us (2%)
    pallas_call x1, Pallas kernels, per_device(): pl.pallas_call(functools.partial(fused, groups, ctx_count, heads, reach),...  112 us
    unnamed x9, local copies, waits for them, and re-layouts  4.46 us

profile of v2, /device:TPU:17, one launch (start us, length us, event | category | flops | bytes accessed | tf_op | source)
XLA Modules:
  0.0 118.2 jit_solution(1975248203356863810)
XLA Ops:
  0.0 0.0 copy-start.1
  0.1 0.8 select_reduce_fusion.1
  0.9 0.7 select_reduce_fusion
  1.7 0.2 and_select_fusion.bias_ref
  1.9 0.0 copy-done.1
  1.9 0.0 copy-start
  1.9 1.6 %copy-done = bf16[512,2048]{1,0:T(8,128)(2,1)S(1)} copy-done((bf16[512,2048]{1,0:T(8,128)(2,1)S(1)}, bf16[512,2048]{1,0:T(8,128)(2,1)}, u32[]{:S(2)}) %copy-start) | copy-done | bytes 2097176
  3.5 0.0 copy-start.2
  3.5 0.9 copy-done.2
  4.5 0.0 copy-start.3
  4.5 0.9 copy-done.3
  5.4 111.8 %shard_map.55 = bf16[256,2048]{1,0:T(8,128)(2,1)S(1)} custom-call(bf16[256,2048]{1,0:T(8,128)(2,1)S(1)} %copy-done.1, bf16[256,512]{1,0:T(8,128)(2,1)S(1)} %copy-done.2, bf16[256,512]{1,0:T(8,128)(2,1)S(1)} %copy-done.3, f32[256,1152]{1,0:T(8,128)S(1)} %and_select_fusion.bias_ref, bf16[512,2048]{1,0:T(8,128)(2,1)S(1)} %copy-done), custom_call_target="tpu_custom_call" | custom-call | tf_op jit(solution)/shard_map/pallas_call | solution.py:304
  117.2 1.0 copy.12
  (8 shorter events, 0.1 us)
Async XLA Ops:
  0.0 1.9 %copy-start.1 = (bf16[256,2048]{1,0:T(8,128)(2,1)S(1)}, bf16[256,2048]{1,0:T(8,128)(2,1)}, u32[]{:S(2)}) copy-start(bf16[256,2048]{1,0:T(8,128)(2,1)} %q_ref.1) | copy-start | bytes 3145732
  1.9 1.6 %copy-start = (bf16[512,2048]{1,0:T(8,128)(2,1)S(1)}, bf16[512,2048]{1,0:T(8,128)(2,1)}, u32[]{:S(2)}) copy-start(bf16[512,2048]{1,0:T(8,128)(2,1)} %w_ref.1) | copy-start | bytes 6291460
  3.5 0.9 copy-start.2
  4.5 0.9 copy-start.3

commit v3 on v2

--- a/solution.py
+++ b/solution.py
@@ -15,8 +15,8 @@
 
 def fused(
     groups, ctx_count, heads, reach,
-    q_ref, k_ref, v_ref, bias_ref, w_ref, out_ref,
-    kv, wbuf, abuf, cbuf, crecv, local_sem,
+    q_hbm, k_hbm, v_hbm, doc_ref, w_ref, out_ref,
+    q_ref, bias_ref, partial, in_sem, kv, wbuf, abuf, cbuf, crecv, local_sem,
     line_send, line_recv, mate_send, mate_recv,
     wmate_send, wmate_recv, wline_send, wline_recv,
     plane_send, plane_recv, core_send, core_recv, c_send, c_recv,
@@ -25,8 +25,8 @@
     x, z = lax.rem(c, 2), c // 2
     lines, steps = ctx_count // 2, reach // 2
     tok = q_ref.shape[0]
-    kv_heads = k_ref.shape[1] // HEAD_SIZE
-    group_width = q_ref.shape[1] // k_ref.shape[1]
+    kv_heads = k_hbm.shape[1] // HEAD_SIZE
+    group_width = q_ref.shape[1] // k_hbm.shape[1]
     chunk = group_width * HEAD_SIZE
     shard = w_ref.shape[0]
     part = wbuf.shape[1]
@@ -47,6 +47,13 @@
         else:
             pl.when(condition)(action)
 
+    loads = [
+        pltpu.make_async_copy(k_hbm, kv.at[0, 0], in_sem.at[0]),
+        pltpu.make_async_copy(v_hbm, kv.at[0, 1], in_sem.at[1]),
+        pltpu.make_async_copy(q_hbm, q_ref, in_sem.at[2]),
+    ]
+    for load in loads:
+        load.start()
     barrier = pltpu.get_barrier_semaphore()
 
     def greet(device):
@@ -78,8 +85,8 @@
     def received(condition, make):
         guarded(condition, lambda: make().wait_recv())
 
-    kv[0, 0] = k_ref[...]
-    kv[0, 1] = v_ref[...]
+    loads[0].wait()
+    loads[1].wait()
 
     def line_copy(s):
         return lambda: copy(
@@ -131,16 +138,34 @@
     def wline_arrives(way, s):
         return z >= s + 1 if way == 0 else z + s + 1 < lines
 
-    def pump_weights(s):
-        for which in range(2):
+    def pump_weights(s, halves):
+        for which in halves:
             for way in range(2):
                 received(wline_arrives(way, s), wline_copy(way, s, which))
                 if s + 1 < lines - 1:
                     start(wline_sends(way, s + 1), wline_copy(way, s + 1, which))
 
     own.wait()
-    for way in (1, 0):
-        start(wline_sends(way, 0), wline_copy(way, 0, 0))
+    start(wline_sends(1, 0), wline_copy(1, 0, 0))
+
+    row = lax.broadcasted_iota(jnp.int32, (BLOCK_TOKENS, BLOCK_TOKENS), 0)
+    col = lax.broadcasted_iota(jnp.int32, (BLOCK_TOKENS, BLOCK_TOKENS), 1)
+    causal = jnp.where(col <= row, 0.0, -1e30).astype(jnp.float32)
+    blocks = tok // BLOCK_TOKENS
+    for d in range(reach + 1):
+        first = 0 if d < reach else blocks - 1
+        for kb in range(first, blocks):
+            key_doc = doc_ref[jnp.maximum((c - d) * blocks + kb, 0)]
+            at = d * tok + (kb - first) * BLOCK_TOKENS
+            for qb in range(blocks):
+                same = (key_doc == doc_ref[c * blocks + qb]) & (c >= d)
+                tile = jnp.zeros_like(causal) + jnp.where(same, 0.0, -1e30).astype(jnp.float32)
+                if d == 0:
+                    tile = jnp.full_like(causal, -1e30) if kb > qb else tile
+                    tile = jnp.minimum(tile, causal) if kb == qb else tile
+                bias_ref[
+                    qb * BLOCK_TOKENS:(qb + 1) * BLOCK_TOKENS, at:at + BLOCK_TOKENS
+                ] = tile
 
     for s in range(1, steps + 1):
         received(z >= s, line_copy(s))
@@ -148,6 +173,8 @@
             start(up & (z >= s), line_copy(s + 1))
             start((x == 0) & (z >= s), mate_copy(s, 0))
         start((x == 1) & (z >= s), mate_copy(s - 1, 1))
+        if s == 1:
+            start(wline_sends(0, 0), wline_copy(0, 0, 0))
     received(None, wmate_copy)
     for way in (1, 0):
         start(wline_sends(way, 0), wline_copy(way, 0, 1))
@@ -191,7 +218,10 @@
             for dh in range(1, heads):
                 start(None, core_copy(hk, i, dh))
 
-    pumped = 0
+    loads[2].wait()
+    last = lines - 2
+    for s in range(last - 1):
+        pump_weights(s, (0, 1))
     for hk in range(kv_heads):
         column = pl.ds(hk * HEAD_SIZE, HEAD_SIZE)
 
@@ -228,16 +258,14 @@
             start(None, plane_copy(hk, i))
         for dh in range(1, heads):
             start(None, core_copy(hk, len(offsets), dh))
-        if hk % 2 == 0 and pumped < lines - 2:
-            pump_weights(pumped)
-            pumped += 1
+        if hk == kv_heads - 2 and last >= 1:
+            pump_weights(last - 1, (0,))
+        if hk == kv_heads - 1 and last >= 1:
+            pump_weights(last - 1, (1,) if kv_heads > 1 else (0, 1))
         if hk >= 2:
             relay(hk - 2)
     for hk in range(max(kv_heads - 2, 0), kv_heads):
         relay(hk)
-    while pumped < lines - 1:
-        pump_weights(pumped)
-        pumped += 1
     for hk in range(kv_heads):
         for i in range(len(offsets) + 1):
             for dh in range(1, heads):
@@ -249,14 +277,24 @@
             return copy(cbuf.at[i], crecv.at[me], c_send.at[i], c_recv.at[i], plane_to(dg, dx))
         return make
 
+    flip = z >= lines // 2
+    far = jnp.where(flip, 0, lines - 1)
+
+    def product(p, source):
+        at = source * shard
+        left = abuf[p, at // chunk, :, pl.ds(pl.multiple_of(lax.rem(at, chunk), shard), shard)]
+        return jnp.dot(left, wbuf[rows_of(source), :], preferred_element_type=jnp.float32)
+
+    for p in range(parts):
+        total = None
+        for source in range(2 * (lines - 1)):
+            term = product(p, source + 2 * flip.astype(jnp.int32))
+            total = term if total is None else total + term
+        partial[p] = total
+    pump_weights(last, (0, 1))
+
     def project(p):
-        total = None
-        for j in range(heads * kv_heads):
-            product = jnp.dot(
-                abuf[p, j], wbuf[j * chunk:(j + 1) * chunk, :], preferred_element_type=jnp.float32
-            )
-            total = product if total is None else total + product
-        return total.astype(jnp.bfloat16)
+        return (partial[p] + product(p, 2 * far) + product(p, 2 * far + 1)).astype(jnp.bfloat16)
 
     for i in reversed(range(len(offsets))):
         dg, dx = offsets[i]
@@ -280,33 +318,21 @@
     parts = 2 * groups
     part = out_weight.shape[1] // parts
     chunk = queries.shape[1] // kv_heads
-    start = lax.axis_index("ctx") * tok
-    query_pos = start + jnp.arange(tok, dtype=jnp.int32)
-    key_pos = jnp.concatenate(
-        [
-            start - d * tok + jnp.arange(0 if d < reach else tok - BLOCK_TOKENS, tok, dtype=jnp.int32)
-            for d in range(reach + 1)
-        ]
-    )
-    table = jnp.arange(doc_of_block.shape[0], dtype=jnp.int32)
-
-    def docs(positions):
-        matches = jnp.floor_divide(positions, BLOCK_TOKENS)[:, None] == table[None, :]
-        return jnp.max(jnp.where(matches, doc_of_block[None, :], -1), axis=1)
-
-    visible = (docs(key_pos)[None, :] == docs(query_pos)[:, None]) & (
-        key_pos[None, :] <= query_pos[:, None]
-    )
-    bias = jnp.where(visible, 0.0, -1e30).astype(jnp.float32)
+    window = reach * tok + BLOCK_TOKENS
     dma = pltpu.SemaphoreType.DMA
     bf16 = jnp.bfloat16
     vmem = pl.BlockSpec(memory_space=pltpu.VMEM)
+    hbm = pl.BlockSpec(memory_space=pl.ANY)
     return pl.pallas_call(
         functools.partial(fused, groups, ctx_count, heads, reach),
         out_shape=jax.ShapeDtypeStruct((tok, out_weight.shape[1]), bf16),
-        in_specs=[vmem, vmem, vmem, vmem, pl.BlockSpec(memory_space=pl.ANY)],
+        in_specs=[hbm, hbm, hbm, pl.BlockSpec(memory_space=pltpu.SMEM), hbm],
         out_specs=vmem,
         scratch_shapes=[
+            pltpu.VMEM(queries.shape, bf16),
+            pltpu.VMEM((tok, window), jnp.float32),
+            pltpu.VMEM((parts, tok, part), jnp.float32),
+            dma((3,)),
             pltpu.VMEM((reach + 1, 2, tok, keys.shape[1]), bf16),
             pltpu.VMEM((ctx_count * out_weight.shape[0], part), bf16),
             pltpu.VMEM((parts, heads * kv_heads, tok, chunk), bf16),
@@ -323,7 +349,7 @@
         compiler_params=pltpu.CompilerParams(
             collective_id=0, has_side_effects=True, vmem_limit_bytes=48 * 1024 * 1024
         ),
-    )(queries, keys, values, bias, out_weight)
+    )(queries, keys, values, doc_of_block, out_weight)
 
 
 def solution(mesh):

time: 120 us -> 123 us (1.025)
  Pallas kernels: 112 us -> 115 us
  local copies, waits for them, and re-layouts: 4.46 us -> 6.34 us
  other arithmetic: 1.86 us -> 0 us
    pallas_call x1, Pallas kernels: 112 us -> 115 us  [per_device(): pl.pallas_call(functools.partial(fused, groups, ctx_count, heads, reach),...]
    unnamed x9 -> x11, local copies, waits for them, and re-layouts: 4.46 us -> 6.34 us
    reduce_max x2 -> x0, other arithmetic: 1.56 us -> none  [docs(): return jnp.max(jnp.where(matches, doc_of_block[None, :], -1), axis=1)]
where the time goes in v3:
time: 123 us; the launch traced here: 122 us
  Pallas kernels  115 us (93%)
  local copies, waits for them, and re-layouts  6.34 us (5%)
    pallas_call x1, Pallas kernels, per_device(): pl.pallas_call(functools.partial(fused, groups, ctx_count, heads, reach),...  115 us
    unnamed x11, local copies, waits for them, and re-layouts  6.34 us

profile of v3, /device:TPU:17, one launch (start us, length us, event | category | flops | bytes accessed | tf_op | source)
XLA Modules:
  0.0 121.6 jit_solution(17469406051448525865)
XLA Ops:
  0.0 0.0 copy-start
  0.0 1.6 %copy-done = bf16[512,2048]{1,0:T(8,128)(2,1)S(1)} copy-done((bf16[512,2048]{1,0:T(8,128)(2,1)S(1)}, bf16[512,2048]{1,0:T(8,128)(2,1)}, u32[]{:S(2)}) %copy-start) | copy-done | bytes 2097176
  1.6 0.0 copy-start.1
  1.6 1.2 %copy-done.1 = bf16[256,2048]{1,0:T(8,128)(2,1)S(1)} copy-done((bf16[256,2048]{1,0:T(8,128)(2,1)S(1)}, bf16[256,2048]{1,0:T(8,128)(2,1)}, u32[]{:S(2)}) %copy-start.1) | copy-done | bytes 1048600
  2.8 0.0 copy-start.2
  2.8 0.9 copy-done.2
  3.8 0.0 copy-start.3
  3.8 0.9 copy-done.3
  4.7 0.0 copy-start.4
  4.7 0.7 copy-done.4
  5.4 115.3 %shard_map.55 = bf16[256,2048]{1,0:T(8,128)(2,1)S(1)} custom-call(bf16[256,2048]{1,0:T(8,128)(2,1)S(1)} %copy-done.1, bf16[256,512]{1,0:T(8,128)(2,1)S(1)} %copy-done.2, bf16[256,512]{1,0:T(8,128)(2,1)S(1)} %copy-done.3, s32[16]{0:T(128)S(1)} %copy-done.4, bf16[512,2048]{1,0:T(8,128)(2,1)S(1)} %copy-done), custom_call_target="tpu_custom_call" | custom-call | tf_op jit(solution)/shard_map/pallas_call | solution.py:326
  120.6 1.0 copy.7
Async XLA Ops:
  0.0 1.6 %copy-start = (bf16[512,2048]{1,0:T(8,128)(2,1)S(1)}, bf16[512,2048]{1,0:T(8,128)(2,1)}, u32[]{:S(2)}) copy-start(bf16[512,2048]{1,0:T(8,128)(2,1)} %w_ref.1) | copy-start | bytes 6291460
  1.6 1.2 %copy-start.1 = (bf16[256,2048]{1,0:T(8,128)(2,1)S(1)}, bf16[256,2048]{1,0:T(8,128)(2,1)}, u32[]{:S(2)}) copy-start(bf16[256,2048]{1,0:T(8,128)(2,1)} %q_hbm.1) | copy-start | bytes 3145732
  2.8 0.9 copy-start.2
  3.8 0.9 copy-start.3
  4.7 0.7 copy-start.4

commit v4 on v3

--- a/solution.py
+++ b/solution.py
@@ -138,15 +138,17 @@
     def wline_arrives(way, s):
         return z >= s + 1 if way == 0 else z + s + 1 < lines
 
-    def pump_weights(s, halves):
+    def pump_weights(s, halves, ways=(1, 0)):
         for which in halves:
-            for way in range(2):
+            for way in ways:
                 received(wline_arrives(way, s), wline_copy(way, s, which))
                 if s + 1 < lines - 1:
                     start(wline_sends(way, s + 1), wline_copy(way, s + 1, which))
 
+    last = lines - 2
     own.wait()
-    start(wline_sends(1, 0), wline_copy(1, 0, 0))
+    for way in (1, 0):
+        start(wline_sends(way, 0), wline_copy(way, 0, 0))
 
     row = lax.broadcasted_iota(jnp.int32, (BLOCK_TOKENS, BLOCK_TOKENS), 0)
     col = lax.broadcasted_iota(jnp.int32, (BLOCK_TOKENS, BLOCK_TOKENS), 1)
@@ -174,10 +176,14 @@
             start((x == 0) & (z >= s), mate_copy(s, 0))
         start((x == 1) & (z >= s), mate_copy(s - 1, 1))
         if s == 1:
-            start(wline_sends(0, 0), wline_copy(0, 0, 0))
-    received(None, wmate_copy)
-    for way in (1, 0):
-        start(wline_sends(way, 0), wline_copy(way, 0, 1))
+            received(None, wmate_copy)
+            for way in (1, 0):
+                start(wline_sends(way, 0), wline_copy(way, 0, 1))
+            if last >= 2:
+                pump_weights(0, (0,), (1,))
+    if last >= 2:
+        pump_weights(0, (1,), (1,))
+        pump_weights(0, (0, 1), (0,))
     for m in range(steps):
         received(c >= 2 * m + 1, mate_copy(m, 0))
     for d in range(1, reach + 1):
@@ -219,8 +225,7 @@
                 start(None, core_copy(hk, i, dh))
 
     loads[2].wait()
-    last = lines - 2
-    for s in range(last - 1):
+    for s in range(1, last - 1):
         pump_weights(s, (0, 1))
     for hk in range(kv_heads):
         column = pl.ds(hk * HEAD_SIZE, HEAD_SIZE)
@@ -258,10 +263,9 @@
             start(None, plane_copy(hk, i))
         for dh in range(1, heads):
             start(None, core_copy(hk, len(offsets), dh))
-        if hk == kv_heads - 2 and last >= 1:
-            pump_weights(last - 1, (0,))
-        if hk == kv_heads - 1 and last >= 1:
-            pump_weights(last - 1, (1,) if kv_heads > 1 else (0, 1))
+        todo = [(way, which) for way in (1, 0) for which in range(2)] if last >= 1 else []
+        for way, which in todo[hk * 4 // kv_heads:(hk + 1) * 4 // kv_heads]:
+            pump_weights(last - 1, (which,), (way,))
         if hk >= 2:
             relay(hk - 2)
     for hk in range(max(kv_heads - 2, 0), kv_heads):

time: 123 us -> 125 us (1.016)
  Pallas kernels: 115 us -> 118 us
    pallas_call x1, Pallas kernels: 115 us -> 118 us  [per_device(): pl.pallas_call(functools.partial(fused, groups, ctx_count, heads, reach),...]
where the time goes in v4:
time: 125 us; the launch traced here: 124 us
  Pallas kernels  118 us (94%)
  local copies, waits for them, and re-layouts  6.34 us (5%)
    pallas_call x1, Pallas kernels, per_device(): pl.pallas_call(functools.partial(fused, groups, ctx_count, heads, reach),...  118 us
    unnamed x11, local copies, waits for them, and re-layouts  6.34 us

profile of v4, /device:TPU:17, one launch (start us, length us, event | category | flops | bytes accessed | tf_op | source)
XLA Modules:
  0.0 124.3 jit_solution(12060292317364949441)
XLA Ops:
  0.0 0.0 copy-start
  0.0 1.6 %copy-done = bf16[512,2048]{1,0:T(8,128)(2,1)S(1)} copy-done((bf16[512,2048]{1,0:T(8,128)(2,1)S(1)}, bf16[512,2048]{1,0:T(8,128)(2,1)}, u32[]{:S(2)}) %copy-start) | copy-done | bytes 2097176
  1.6 0.0 copy-start.1
  1.6 1.2 copy-done.1
  2.8 0.0 copy-start.2
  2.8 0.9 copy-done.2
  3.8 0.0 copy-start.3
  3.8 0.9 copy-done.3
  4.7 0.0 copy-start.4
  4.7 0.7 copy-done.4
  5.4 118.0 %shard_map.55 = bf16[256,2048]{1,0:T(8,128)(2,1)S(1)} custom-call(bf16[256,2048]{1,0:T(8,128)(2,1)S(1)} %copy-done.1, bf16[256,512]{1,0:T(8,128)(2,1)S(1)} %copy-done.2, bf16[256,512]{1,0:T(8,128)(2,1)S(1)} %copy-done.3, s32[16]{0:T(128)S(1)} %copy-done.4, bf16[512,2048]{1,0:T(8,128)(2,1)S(1)} %copy-done), custom_call_target="tpu_custom_call" | custom-call | tf_op jit(solution)/shard_map/pallas_call | solution.py:330
  123.3 1.0 copy.7
Async XLA Ops:
  0.0 1.6 %copy-start = (bf16[512,2048]{1,0:T(8,128)(2,1)S(1)}, bf16[512,2048]{1,0:T(8,128)(2,1)}, u32[]{:S(2)}) copy-start(bf16[512,2048]{1,0:T(8,128)(2,1)} %w_ref.1) | copy-start | bytes 6291460
  1.6 1.2 copy-start.1
  2.8 0.9 copy-start.2
  3.8 0.9 copy-start.3
  4.7 0.7 copy-start.4
